TPU v7x, 32 devices: a whole 2x2x4 slice. The times are simulated.
32 devices in a mesh: lang: 2 (over y), fsdp: 16 (over z, x, core).
Axes of the slice: x: 2, y: 2, z: 4, core: 2. Of those that a mesh axis runs over, the one named last changes fastest.
Arguments:
- tokens: bfloat16 [2, 768, 8192], P('lang', 'fsdp'), may hold values from -6 to 6
- grad_out: bfloat16 [2, 768, 8192], P('lang', 'fsdp'), may hold values from -24 to 24
- doc_ids: int32 [2, 768], P('lang'), may hold values from 0 to 95, never falling along the last dimension, each value on 1 to 64 neighbouring positions
- w_gate: bfloat16 [8192, 4096], P(None, 'fsdp'), may hold values from -0.0625 to 0.0625
- w_up: bfloat16 [8192, 4096], P(None, 'fsdp'), may hold values from -0.0625 to 0.0625
- w_down: bfloat16 [4096, 8192], P('fsdp'), may hold values from -0.09375 to 0.09375
Outputs:
- grad_tokens: bfloat16 [2, 768, 8192], P('lang', 'fsdp')
- grad_gate: bfloat16 [8192, 4096], P('lang', 'fsdp')
- grad_up: bfloat16 [8192, 4096], P('lang', 'fsdp')
- grad_down: bfloat16 [4096, 8192], P('fsdp', 'lang')
Inputs may be any that keep to these rules, and one draw needn't show every extreme that they name: `doc_ids`: document numbers never fall along a group's pack.
All inputs are finite; a program needn't handle non-finite values.
Results may differ from a plain program's by a relative error of at most 0.015.
Values may be sent and summed in bfloat16 or wider, within the bound.
A program may use at most 192 MiB of HBM per device.

v0:
```python
import jax
import jax.numpy as jnp
from jax import lax
from jax.sharding import PartitionSpec as P

epsilon = 1e-06


def contract_rows(left, right):
    return lax.dot_general(
        left, right, (((0,), (0,)), ((), ())), preferred_element_type=jnp.float32
    )


def contract_cols(left, right):
    return lax.dot_general(
        left, right, (((1,), (1,)), ((), ())), preferred_element_type=jnp.float32
    )


def body(tokens, grad_out, doc_ids, w_gate, w_up, w_down):
    features, upstream = (
        lax.all_gather(tokens, "fsdp", axis=1, tiled=True),
        lax.all_gather(grad_out, "fsdp", axis=1, tiled=True),
    )
    features = features[0]
    upstream = upstream[0]
    segment = doc_ids[0]
    width = features.shape[1]
    counts = jnp.sum((segment[:, None] == segment[None, :]).astype(jnp.float32), axis=1)
    inverse = 1.0 / counts
    gate_pre = jnp.dot(features, w_gate, preferred_element_type=jnp.float32)
    up_pre = jnp.dot(features, w_up, preferred_element_type=jnp.float32)
    gate_sig = jax.nn.sigmoid(gate_pre)
    activated = gate_pre * gate_sig
    hidden = (activated * up_pre * inverse[:, None]).astype(jnp.bfloat16)
    hid_grad = contract_cols(upstream, w_down) * inverse[:, None]
    gate_grad = (hid_grad * up_pre * gate_sig * (1.0 + gate_pre * (1.0 - gate_sig))).astype(
        jnp.bfloat16
    )
    up_grad = (hid_grad * activated).astype(jnp.bfloat16)
    stacked = jnp.stack(
        [
            contract_rows(features, gate_grad),
            contract_rows(features, up_grad),
            contract_rows(upstream, hidden),
        ]
    )
    moment = jnp.sum(stacked * stacked, axis=(0, 1)) / (3.0 * width) + epsilon
    ratios = 1.0 / moment
    every_ratio = lax.all_gather(ratios[None], "lang", axis=0, tiled=True)
    summed_ratio = jnp.sum(every_ratio, axis=0)
    weighted = stacked * (ratios / summed_ratio)[None, None, :]
    shares = lax.psum_scatter(
        weighted.astype(jnp.bfloat16), "lang", scatter_dimension=1, tiled=True
    ).astype(jnp.float32)
    grad_gate = shares[0].astype(jnp.bfloat16)
    grad_up = shares[1].astype(jnp.bfloat16)
    grad_down = shares[2].T.astype(jnp.bfloat16)
    summed = lax.psum_scatter(
        (contract_cols(gate_grad, w_gate) + contract_cols(up_grad, w_up)).astype(jnp.bfloat16),
        "fsdp",
        scatter_dimension=0,
        tiled=True,
    )
    grad_tokens = summed[None]
    return (grad_tokens, grad_gate, grad_up, grad_down)


def solution(mesh):
    return jax.shard_map(
        body,
        mesh=mesh,
        in_specs=(
            P("lang", "fsdp", None),
            P("lang", "fsdp", None),
            P("lang", None),
            P(None, "fsdp"),
            P(None, "fsdp"),
            P("fsdp", None),
        ),
        out_specs=(
            P("lang", "fsdp", None),
            P("lang", "fsdp"),
            P("lang", "fsdp"),
            P("fsdp", "lang"),
        ),
        check_vma=False,
    )
```

profile of v0, /device:TPU:0, one launch (start us, length us, event | category | flops | bytes accessed | tf_op | source)
XLA Modules:
  0.0 565.1 jit_solution(17670347876107671347)
XLA Ops:
  7.2 0.7 all-gather.7.cloned.1.call-update
  7.9 0.7 all-gather.5.cloned.1.call-update
  8.7 0.7 reduce.1
  9.8 104.0 %all-gather.7.cloned.1.call-done = bf16[1,768,8192]{2,1,0:T(8,128)(2,1)} async-done(((bf16[1,48,8192]{2,1,0:T(8,128)(2,1)}), bf16[1,768,8192]{2,1,0:T(8,128)(2,1)}) %all-gather.7.cloned.1.call-update) | async-done | bytes 12582928 | tf_op jit(solution)/shard_map/all_gather | solution.py:23
  113.8 7.8 %fusion.4 = f32[768,256]{1,0:T(8,128)S(1)} fusion(bf16[8192,256]{1,0:T(8,128)(2,1)} %param.9, bf16[1,768,8192]{2,1,0:T(8,128)(2,1)} %all-gather.7.cloned.1.call-done), kind=kOutput, calls=%fused_computation.8 | convolution fusion | flops 3221225472 | bytes 17563648 | tf_op jit(solution)/shard_map/dot_general | solution.py:32
  121.5 2.2 copy-done.2
  123.7 1.4 copy-done.4
  125.1 3.4 fusion.6
  128.6 86.5 %all-gather.5.cloned.1.call-done = bf16[1,768,8192]{2,1,0:T(8,128)(2,1)} async-done(((bf16[1,48,8192]{2,1,0:T(8,128)(2,1)}), bf16[1,768,8192]{2,1,0:T(8,128)(2,1)}) %all-gather.5.cloned.1.call-update) | async-done | bytes 12582928 | tf_op jit(solution)/shard_map/all_gather | solution.py:24
  215.0 7.1 %fusion.12 = f32[1,8192,256]{1,2,0:T(8,128)S(1)} fusion(bf16[1,768,8192]{2,1,0:T(8,128)(2,1)} %all-gather.5.cloned.1.call-done, f32[768,256]{1,0:T(8,128)S(1)} %fusion.6, f32[768]{0:T(1024)S(1)} %broadcast_divide_fusion, f32[768,256]{1,0:T(8,128)S(1)} %fusion.4), kind=kOutput, calls=%fused_computation.16 | convolution fusion | flops 3222601728 | bytes 22547456 | tf_op jit(solution)/shard_map/dot_general | solution.py:10
  222.1 1.1 copy-done.3
  223.2 8.9 %multiply_convert_fusion.2 = (bf16[768,256]{1,0:T(8,128)(2,1)S(1)}, bf16[768,256]{1,0:T(8,128)(2,1)S(1)}) fusion(f32[768,256]{1,0:T(8,128)S(1)} %fusion.4, f32[768,256]{1,0:T(8,128)S(1)} %fusion.6, f32[768]{0:T(1024)S(1)} %broadcast_divide_fusion, bf16[256,8192]{1,0:T(8,128)(2,1)} %param.11, bf16[1,768,8192]{2,1,0:T(8,128)(2,1)S(1)} %copy-done.3), kind=kOutput, calls=%fused_computation.25 | convolution fusion | flops 3223977984 | bytes 19139584 | tf_op jit(solution)/shard_map/dot_general | solution.py:16
  232.1 6.7 %fusion.18 = f32[1,8192,256]{1,2,0:T(8,128)S(1)} fusion(bf16[768,256]{1,0:T(8,128)(2,1)S(1)} %get-tuple-element.19, bf16[1,768,8192]{2,1,0:T(8,128)(2,1)} %all-gather.7.cloned.1.call-done), kind=kOutput, calls=%fused_computation.18 | convolution fusion | flops 3221225472 | bytes 21364736 | tf_op jit(solution)/shard_map/dot_general | solution.py:10
  238.8 13.4 %fusion.15 = f32[1,8192,256]{1,2,0:T(8,128)} fusion(bf16[768,256]{1,0:T(8,128)(2,1)S(1)} %get-tuple-element.20, bf16[1,768,8192]{2,1,0:T(8,128)(2,1)} %all-gather.7.cloned.1.call-done), kind=kOutput, calls=%fused_computation.17 | convolution fusion | flops 3221225472 | bytes 21364736 | tf_op jit(solution)/shard_map/dot_general | solution.py:10
  252.2 6.2 %multiply_reduce_fusion = f32[256]{0:T(256)S(1)} fusion(f32[1,8192,256]{1,2,0:T(8,128)S(1)} %fusion.12, f32[1,8192,256]{1,2,0:T(8,128)S(1)} %fusion.18, f32[1,8192,256]{1,2,0:T(8,128)} %fusion.15), kind=kLoop, calls=%fused_computation.2 | loop fusion | flops 25165568 | bytes 25166848 | tf_op jit(solution)/shard_map/reduce_sum | solution.py:49
  258.4 4.2 all-gather.1
  262.7 13.7 %multiply_convert_fusion = bf16[3,8192,256]{1,2,0:T(8,128)(2,1)} fusion(f32[1,8192,256]{1,2,0:T(8,128)} %copy-done, f32[1,8192,256]{1,2,0:T(8,128)} %copy-done.1, f32[1,8192,256]{1,2,0:T(8,128)} %fusion.15, f32[256]{0:T(256)S(1)} %multiply_divide_fusion), kind=kLoop, calls=%fused_computation.1 | loop fusion | flops 25165824 | bytes 37749760 | tf_op jit(solution)/shard_map/convert_element_type | solution.py:55
  276.5 12.6 %fusion.29 = f32[768,8192]{1,0:T(8,128)} fusion(bf16[768,256]{1,0:T(8,128)(2,1)S(1)} %get-tuple-element.20, bf16[8192,256]{1,0:T(8,128)(2,1)} %param.9), kind=kOutput, calls=%fused_computation.35 | convolution fusion | flops 3221225472 | bytes 29753344 | tf_op jit(solution)/shard_map/dot_general | solution.py:16
  289.1 15.9 %add_convert_fusion = bf16[768,8192]{1,0:T(8,128)(2,1)} fusion(f32[768,8192]{1,0:T(8,128)} %fusion.29, bf16[768,256]{1,0:T(8,128)(2,1)S(1)} %get-tuple-element.19, bf16[8192,256]{1,0:T(8,128)(2,1)} %param.10), kind=kOutput, calls=%fused_computation.3 | convolution fusion | flops 3233808384 | bytes 42336256 | tf_op jit(solution)/shard_map/dot_general | solution.py:16
  305.1 114.2 %reduce-scatter.5.cloned.1.call-done = bf16[3,4096,256]{1,2,0:T(8,128)(2,1)} async-done(((bf16[3,8192,256]{1,2,0:T(8,128)(2,1)}), bf16[3,4096,256]{1,2,0:T(8,128)(2,1)}) %reduce-scatter.5.cloned.1.call-update) | async-done | bytes 6291472 | tf_op jit(solution)/shard_map/reduce_scatter | solution.py:54
  419.3 5.5 slice_bitcast_fusion
  424.8 4.1 copy.15
  428.9 2.4 copy.14
  431.3 127.2 %reduce-scatter.3.cloned.1.call-done = bf16[48,8192]{1,0:T(8,128)(2,1)} async-done(((bf16[768,8192]{1,0:T(8,128)(2,1)}), bf16[48,8192]{1,0:T(8,128)(2,1)}) %reduce-scatter.3.cloned.1.call-update) | async-done | bytes 786448 | tf_op jit(solution)/shard_map/reduce_scatter | solution.py:60
  (18 shorter events, 0.6 us)
Async XLA Ops:
  7.2 106.6 %all-gather.7.cloned.1.call-start = ((), (), s32[]{:S(2)}) async-start(), calls=%async_computation.3 | async-start | bytes 13369344 | tf_op jit(solution)/shard_map/all_gather | solution.py:23
  7.9 207.1 %all-gather.5.cloned.1.call-start = ((), (), s32[]{:S(2)}) async-start(), calls=%async_computation.2 | async-start | bytes 13369344 | tf_op jit(solution)/shard_map/all_gather | solution.py:24
  8.6 410.6 %reduce-scatter.5.cloned.1.call-start = ((), (), s32[]{:S(2)}) async-start(), calls=%async_computation.5 | async-start | bytes 18874368 | tf_op jit(solution)/shard_map/reduce_scatter | solution.py:54
  113.8 9.9 %copy-start.2 = (bf16[1,768,8192]{2,1,0:T(8,128)(2,1)S(1)}, bf16[1,768,8192]{2,1,0:T(8,128)(2,1)}, u32[]{:S(2)}) copy-start(bf16[1,768,8192]{2,1,0:T(8,128)(2,1)} %all-gather.7.cloned.1.call-done) | copy-start | bytes 37748740
  113.8 11.4 %copy-start.4 = (bf16[8192,256]{1,0:T(8,128)(2,1)S(1)}, bf16[8192,256]{1,0:T(8,128)(2,1)}, u32[]{:S(2)}) copy-start(bf16[8192,256]{1,0:T(8,128)(2,1)} %param.10) | copy-start | bytes 12582916
  215.0 8.2 %copy-start.3 = (bf16[1,768,8192]{2,1,0:T(8,128)(2,1)S(1)}, bf16[1,768,8192]{2,1,0:T(8,128)(2,1)}, u32[]{:S(2)}) copy-start(bf16[1,768,8192]{2,1,0:T(8,128)(2,1)} %all-gather.5.cloned.1.call-done) | copy-start | bytes 37748740
  223.2 29.0 %copy-start = (f32[1,8192,256]{1,2,0:T(8,128)}, f32[1,8192,256]{1,2,0:T(8,128)S(1)}, u32[]{:S(2)}) copy-start(f32[1,8192,256]{1,2,0:T(8,128)S(1)} %fusion.12) | copy-start | bytes 25165828
  238.8 13.5 %copy-start.1 = (f32[1,8192,256]{1,2,0:T(8,128)}, f32[1,8192,256]{1,2,0:T(8,128)S(1)}, u32[]{:S(2)}) copy-start(f32[1,8192,256]{1,2,0:T(8,128)S(1)} %fusion.18) | copy-start | bytes 25165828
  276.5 282.1 %reduce-scatter.3.cloned.1.call-start = ((), (), s32[]{:S(2)}) async-start(), calls=%async_computation.4 | async-start | bytes 13369344 | tf_op jit(solution)/shard_map/reduce_scatter | solution.py:60
Sparse Core Ops, SparseCore 0:
  10.3 103.4 all-gather.6
  116.1 98.9 all-gather.4
  276.6 142.6 reduce-scatter.4
  423.8 134.7 reduce-scatter.2
where the time goes:
time: 566 us; the launch traced here: 565 us
  waiting for transfers between devices  433 us (77%)
  matrix products  75.8 us (13%)
  other arithmetic  21.1 us (4%)
  local copies, waits for them, and re-layouts  16.7 us (3%)
  between operations  13.8 us (2%)
    reduce_scatter x1, waiting for transfers between devices, body(): lax.psum_scatter((contract_cols(gate_grad, w_gate) + contract_cols(up_gra...  127 us
    reduce_scatter x1, waiting for transfers between devices, body(): lax.psum_scatter(weighted.astype(jnp.bfloat16), 'lang', scatter_dimension...  114 us
    all_gather x1, waiting for transfers between devices, body(): lax.all_gather(tokens, 'fsdp', axis=1, tiled=True)  104 us
    all_gather x1, waiting for transfers between devices, body(): lax.all_gather(grad_out, 'fsdp', axis=1, tiled=True)  86.5 us
    dot_general x3, matrix products, contract_cols(): lax.dot_general(left, right, (((1,), (1,)), ((), ())), preferred_element_...  37.4 us
    dot_general x3, matrix products, contract_rows(): lax.dot_general(left, right, (((0,), (0,)), ((), ())), preferred_element_...  27.2 us
    convert_element_type x1, other arithmetic, body(): weighted.astype(jnp.bfloat16)  13.7 us
  transfers between devices with their start and end apart: 4, of which 4 were waited for; matrix products, arithmetic and copies ran while one was open for 9% of the time, Pallas kernels for 0%

commit v1 on v0

v1 whole, which is shorter than its diff:
```python
import functools

import jax
import jax.numpy as jnp
from jax import lax
from jax.experimental import pallas as pl
from jax.experimental.pallas import tpu as pltpu
from jax.sharding import PartitionSpec as P

epsilon = 1e-06
CORES = 2


def contract_rows(left, right):
    return lax.dot_general(
        left, right, (((0,), (0,)), ((), ())), preferred_element_type=jnp.float32
    )


def contract_cols(left, right):
    return lax.dot_general(
        left, right, (((1,), (1,)), ((), ())), preferred_element_type=jnp.float32
    )


def chip_of(position, chips):
    back = position // (chips // 2)
    return (1 - back) * 2 * position + back * (2 * (chips - 1 - position) + 1)


def position_of(chip, chips):
    odd = chip % 2
    return (1 - odd) * (chip // 2) + odd * (chips - 1 - chip // 2)


def gather_kernel(
    langs, shards, tok_ref, up_ref, tok_out, up_out,
    ring_send, ring_recv, sib_send, sib_recv, lang_send, lang_recv, local_sem,
):
    chips = shards // CORES
    rows = tok_ref.shape[0]
    width = tok_ref.shape[1] // langs
    lang = lax.axis_index("lang")
    me = lax.axis_index("fsdp")
    core = me % CORES
    place = position_of(me // CORES, chips)
    right = chip_of((place + 1) % chips, chips) * CORES + core
    left = chip_of((place + chips - 1) % chips, chips) * CORES + core
    sibling = me + 1 - 2 * core

    barrier = pltpu.get_barrier_semaphore()
    peers = [(lang, right), (lang, left), (lang, sibling)]
    peers += [((lang + d) % langs, me) for d in range(1, langs)]
    for peer in peers:
        pl.semaphore_signal(barrier, inc=1, device_id=peer, device_id_type=pl.DeviceIdType.MESH)
    pl.semaphore_wait(barrier, len(peers))

    ins = (tok_ref, up_ref)
    outs = (tok_out, up_out)
    nexts = (right, left)

    def block(array, group, shard):
        return outs[array].at[group, pl.ds(pl.multiple_of(shard * rows, rows), rows), :]

    def own(array, group):
        return ins[array].at[:, pl.ds(pl.multiple_of(group * width, width), width)]

    def remote(src, dst, send, recv, device):
        return pltpu.make_async_remote_copy(
            src_ref=src, dst_ref=dst, send_sem=send, recv_sem=recv,
            device_id=device, device_id_type=pl.DeviceIdType.MESH,
        )

    def origin(array, step):
        shift = chips - step if array == 0 else step
        return chip_of((place + shift) % chips, chips) * CORES + core

    sends = []
    locals_ = []
    lang_copies = {}
    for array in range(2):
        for d in range(1, langs):
            peer = (lang + d) % langs
            copy = remote(
                own(array, peer), block(array, lang, me),
                lang_send.at[array, d], lang_recv.at[array, d], (peer, me),
            )
            copy.start()
            lang_copies[array, d] = copy
    for array in range(2):
        copy = pltpu.make_async_copy(own(array, lang), block(array, lang, me), local_sem.at[array])
        copy.start()
        locals_.append(copy)

    ring = {}
    sib = {}

    def forward(array, d, step, src):
        group = (lang + langs - d) % langs
        shard = origin(array, step)
        dst = block(array, group, shard)
        if step < chips - 1:
            copy = remote(
                src, dst, ring_send.at[array, d, step], ring_recv.at[array, d, step],
                (lang, nexts[array]),
            )
            copy.start()
            ring[array, d, step] = copy
        copy = remote(
            src, dst, sib_send.at[array, d, step], sib_recv.at[array, d, step], (lang, sibling)
        )
        copy.start()
        sib[array, d, step] = copy

    for step in range(chips):
        for d in range(langs):
            for array in range(2):
                group = (lang + langs - d) % langs
                if step == 0:
                    if d == 0:
                        src = own(array, lang)
                    else:
                        lang_copies[array, d].wait_recv()
                        src = block(array, group, me)
                else:
                    ring[array, d, step - 1].wait_recv()
                    src = block(array, group, origin(array, step))
                forward(array, d, step, src)
    for copy in locals_:
        copy.wait()
    for copy in lang_copies.values():
        copy.wait_send()
    for copy in ring.values():
        copy.wait_send()
    for copy in sib.values():
        copy.wait()


def gather(tokens, grad_out, langs, shards):
    rows, width = tokens.shape
    chips = shards // CORES
    out = jax.ShapeDtypeStruct((langs, rows * shards, width // langs), tokens.dtype)
    dma = pltpu.SemaphoreType.DMA
    return pl.pallas_call(
        functools.partial(gather_kernel, langs, shards),
        out_shape=(out, out),
        in_specs=[pl.BlockSpec(memory_space=pl.ANY)] * 2,
        out_specs=(pl.BlockSpec(memory_space=pl.ANY),) * 2,
        scratch_shapes=[
            dma((2, langs, chips)), dma((2, langs, chips)),
            dma((2, langs, chips)), dma((2, langs, chips)),
            dma((2, langs)), dma((2, langs)), dma((2,)),
        ],
        compiler_params=pltpu.CompilerParams(collective_id=0, has_side_effects=True),
        name="gather",
    )(tokens, grad_out)


def scatter_kernel(
    langs, shards, part_ref, out_ref, mine, sib_in, ring_in,
    load_sem, sib_send, sib_recv, ring_send, ring_recv, lang_send, lang_recv, local_sem,
):
    chips = shards // CORES
    rows, width = mine.shape[2:]
    lang = lax.axis_index("lang")
    me = lax.axis_index("fsdp")
    core = me % CORES
    place = position_of(me // CORES, chips)
    right = chip_of((place + 1) % chips, chips) * CORES + core
    left = chip_of((place + chips - 1) % chips, chips) * CORES + core
    sibling = me + 1 - 2 * core

    barrier = pltpu.get_barrier_semaphore()
    peers = [(lang, right), (lang, left), (lang, sibling)]
    peers += [((lang + d) % langs, me) for d in range(1, langs)]
    for peer in peers:
        pl.semaphore_signal(barrier, inc=1, device_id=peer, device_id_type=pl.DeviceIdType.MESH)
    pl.semaphore_wait(barrier, len(peers))

    def remote(src, dst, send, recv, device):
        return pltpu.make_async_remote_copy(
            src_ref=src, dst_ref=dst, send_sem=send, recv_sem=recv,
            device_id=device, device_id_type=pl.DeviceIdType.MESH,
        )

    def piece(d, step, own):
        shift = step + 1 if d % 2 else chips - 1 - step
        chip = chip_of((place + shift) % chips, chips)
        shard = chip * CORES + (core if own else 1 - core)
        start = ((lang + d) % langs) * (shards * rows) + shard * rows
        return part_ref.at[pl.ds(pl.multiple_of(start, rows), rows), :]

    loads, sib, ring = {}, {}, {}
    order = [(step, d) for step in range(chips) for d in range(langs)]
    for step, d in order:
        sib[d, step] = remote(
            piece(d, step, False), sib_in.at[d, step],
            sib_send.at[d, step], sib_recv.at[d, step], (lang, sibling),
        )
        sib[d, step].start()
        loads[d, step] = pltpu.make_async_copy(
            piece(d, step, True), mine.at[d, step], load_sem.at[d, step]
        )
        loads[d, step].start()
    tail = []
    for step, d in order:
        loads[d, step].wait()
        sib[d, step].wait_recv()
        total = mine[d, step].astype(jnp.float32) + sib_in[d, step].astype(jnp.float32)
        if step:
            ring[d, step - 1].wait_recv()
            total = total + ring_in[d, step - 1].astype(jnp.float32)
        mine[d, step] = total.astype(mine.dtype)
        if step < chips - 1:
            ring[d, step] = remote(
                mine.at[d, step], ring_in.at[d, step],
                ring_send.at[d, step], ring_recv.at[d, step],
                (lang, left if d % 2 else right),
            )
            ring[d, step].start()
        else:
            dst = out_ref.at[:, pl.ds(pl.multiple_of(lang * width, width), width)]
            if d == 0:
                copy = pltpu.make_async_copy(mine.at[d, step], dst, local_sem)
            else:
                copy = remote(
                    mine.at[d, step], dst, lang_send.at[d], lang_recv.at[d],
                    ((lang + d) % langs, me),
                )
            copy.start()
            tail.append(copy)
    for copy in tail:
        copy.wait()
    for copy in list(sib.values()) + list(ring.values()):
        copy.wait_send()


def scatter(partial, langs, shards):
    width = partial.shape[1]
    rows = partial.shape[0] // (langs * shards)
    chips = shards // CORES
    dma = pltpu.SemaphoreType.DMA
    return pl.pallas_call(
        functools.partial(scatter_kernel, langs, shards),
        out_shape=jax.ShapeDtypeStruct((rows, width * langs), partial.dtype),
        in_specs=[pl.BlockSpec(memory_space=pl.ANY)],
        out_specs=pl.BlockSpec(memory_space=pl.ANY),
        scratch_shapes=[
            pltpu.VMEM((langs, chips, rows, width), partial.dtype),
            pltpu.VMEM((langs, chips, rows, width), partial.dtype),
            pltpu.VMEM((langs, chips, rows, width), partial.dtype),
            dma((langs, chips)), dma((langs, chips)), dma((langs, chips)),
            dma((langs, chips)), dma((langs, chips)), dma((langs,)), dma((langs,)), dma,
        ],
        compiler_params=pltpu.CompilerParams(
            collective_id=1, has_side_effects=True, vmem_limit_bytes=40 * 2**20
        ),
        name="scatter",
    )(partial)


def swap_sum(value, langs):
    sent = value.astype(jnp.bfloat16)
    total = value
    for d in range(1, langs):
        got = lax.ppermute(sent, "lang", [(i, (i + d) % langs) for i in range(langs)])
        total = total + got.astype(jnp.float32)
    return total


def body(langs, shards, tokens, grad_out, doc_ids, w_gate, w_up, w_down):
    lang = lax.axis_index("lang")
    depth = w_gate.shape[0]
    width = depth // langs
    feats, ups = gather(tokens[0], grad_out[0], langs, shards)
    count_tokens = feats.shape[1]
    feats = feats.reshape(langs * count_tokens, width)
    ups = ups.reshape(langs * count_tokens, width)
    segment = doc_ids[0]
    counts = jnp.sum((segment[:, None] == segment[None, :]).astype(jnp.float32), axis=1)
    inverse = lax.all_gather(1.0 / counts, "lang", axis=0, tiled=True)[:, None]
    wg = lax.dynamic_slice_in_dim(w_gate, lang * width, width, 0)
    wu = lax.dynamic_slice_in_dim(w_up, lang * width, width, 0)
    wd = lax.dynamic_slice_in_dim(w_down, lang * width, width, 1)
    gate_pre = swap_sum(jnp.dot(feats, wg, preferred_element_type=jnp.float32), langs)
    up_pre = swap_sum(jnp.dot(feats, wu, preferred_element_type=jnp.float32), langs)
    hid_grad = swap_sum(contract_cols(ups, wd), langs) * inverse
    gate_sig = jax.nn.sigmoid(gate_pre)
    activated = gate_pre * gate_sig
    hidden = (activated * up_pre * inverse).astype(jnp.bfloat16)
    gate_grad = (hid_grad * up_pre * gate_sig * (1.0 + gate_pre * (1.0 - gate_sig))).astype(
        jnp.bfloat16
    )
    up_grad = (hid_grad * activated).astype(jnp.bfloat16)

    partial = contract_cols(
        jnp.concatenate([gate_grad, up_grad], axis=1), jnp.concatenate([wg, wu], axis=1)
    ).astype(jnp.bfloat16)
    grad_tokens = scatter(partial, langs, shards)[None]

    def by_lang(left, right):
        left = left.reshape(langs, count_tokens, -1)
        right = right.reshape(langs, count_tokens, -1)
        return [contract_rows(left[l], right[l]) for l in range(langs)]

    g_gate = by_lang(feats, gate_grad)
    g_up = by_lang(feats, up_grad)
    g_down = by_lang(hidden, ups)
    squares = jnp.stack([
        jnp.sum(g_gate[l] ** 2, axis=0) + jnp.sum(g_up[l] ** 2, axis=0) + jnp.sum(g_down[l] ** 2, axis=1)
        for l in range(langs)
    ])
    moment = lax.psum(squares, "lang") / (3.0 * depth) + epsilon
    ratios = 1.0 / moment
    share = ratios / jnp.sum(ratios, axis=0, keepdims=True)

    def weigh(parts, axis):
        total = 0.0
        for l in range(langs):
            total = total + parts[l] * (share[l][None, :] if axis else share[l][:, None])
        return total.astype(jnp.bfloat16)

    return grad_tokens, weigh(g_gate, 1), weigh(g_up, 1), weigh(g_down, 0)


def solution(mesh):
    return jax.shard_map(
        functools.partial(body, mesh.shape["lang"], mesh.shape["fsdp"]),
        mesh=mesh,
        in_specs=(
            P("lang", "fsdp", None),
            P("lang", "fsdp", None),
            P("lang", None),
            P(None, "fsdp"),
            P(None, "fsdp"),
            P("fsdp", None),
        ),
        out_specs=(
            P("lang", "fsdp", None),
            P("lang", "fsdp"),
            P("lang", "fsdp"),
            P("fsdp", "lang"),
        ),
        check_vma=False,
    )
```

time: 566 us -> 343 us (0.61)
  waiting for transfers between devices: 433 us -> 0.01 us
  Pallas kernels: 0 us -> 213 us
  blocking collectives: 4.25 us -> 38.7 us
  between operations: 13.8 us -> 0.82 us
  local copies, waits for them, and re-layouts: 16.7 us -> 5.79 us
  matrix products: 75.8 us -> 65.8 us
    reduce_scatter x2 -> x0, waiting for transfers between devices: 241 us -> none  [the longest x1 127 us: body(): lax.psum_scatter((contract_cols(gate_grad, w_gate) + contract_cols(up_gra...]
    pallas_call x0 -> x2, Pallas kernels: none -> 213 us  [the longest x1 136 us: gather(): pl.pallas_call(functools.partial(gather_kernel, langs, shards), out_shape...]
    all_gather x2 -> x0, waiting for transfers between devices: 190 us -> none  [the longest x1 104 us: body(): lax.all_gather(tokens, 'fsdp', axis=1, tiled=True)]
    all_gather x1, blocking collectives: 4.25 us -> 33.7 us  [body(): inverse = lax.all_gather(1.0 / counts, 'lang', axis=0, tiled=True)[:, None]]
    dot_general x3 -> x2, matrix products: 37.4 us -> 19.9 us  [contract_cols(): lax.dot_general(left, right, (((1,), (1,)), ((), ())), preferred_element_...]
    reduce_sum x2 -> x1, other arithmetic: 6.22 us -> 0.03 us  [body(): share = ratios / jnp.sum(ratios, axis=0, keepdims=True)]
    dot_general x2, matrix products: 11.2 us -> 16.9 us  [the longest x1 8.75 us: body(): jnp.dot(feats, wu, preferred_element_type=jnp.float32)]
    unnamed x12 -> x25, local copies, waits for them, and re-layouts: 11.2 us -> 5.51 us
  transfers between devices with their start and end apart: 4 -> 3, of which waited for: 4 -> 0; matrix products, arithmetic and copies ran while one was open for 9% -> 5% of each run, Pallas kernels for 0% -> 0%
where the time goes in v1:
time: 343 us
  Pallas kernels  213 us (62%)
  matrix products  65.8 us (19%)
  blocking collectives  38.7 us (11%)
  other arithmetic  16.1 us (5%)
  local copies, waits for them, and re-layouts  5.79 us (2%)
    pallas_call x1, Pallas kernels, gather(): pl.pallas_call(functools.partial(gather_kernel, langs, shards), out_shape...  136 us
    pallas_call x1, Pallas kernels, scatter(): pl.pallas_call(functools.partial(scatter_kernel, langs, shards), out_shap...  76.7 us
    all_gather x1, blocking collectives, body(): inverse = lax.all_gather(1.0 / counts, 'lang', axis=0, tiled=True)[:, None]  33.7 us
    dot_general x6, matrix products, contract_rows(): lax.dot_general(left, right, (((0,), (0,)), ((), ())), preferred_element_...  29 us
    dot_general x2, matrix products, contract_cols(): lax.dot_general(left, right, (((1,), (1,)), ((), ())), preferred_element_...  19.9 us
    convert_element_type x2, other arithmetic, weigh(): return total.astype(jnp.bfloat16)  11.6 us
    dot_general x1, matrix products, body(): jnp.dot(feats, wu, preferred_element_type=jnp.float32)  8.75 us
    dot_general x1, matrix products, body(): jnp.dot(feats, wg, preferred_element_type=jnp.float32)  8.12 us
  transfers between devices with their start and end apart: 3, of which 0 were waited for; matrix products, arithmetic and copies ran while one was open for 5% of the time, Pallas kernels for 0%

profile of v1, /device:TPU:0, one launch (start us, length us, event | category | flops | bytes accessed | tf_op | source)
XLA Modules:
  0.0 342.8 jit_solution(13541169425994624928)
XLA Ops:
  0.6 136.4 %gather.1 = (bf16[2,768,4096]{2,1,0:T(8,128)(2,1)}, bf16[2,768,4096]{2,1,0:T(8,128)(2,1)}) custom-call(bf16[48,8192]{1,0:T(8,128)(2,1)} %bitcast.43, bf16[48,8192]{1,0:T(8,128)(2,1)} %bitcast.44), custom_call_target="tpu_custom_call" | custom-call | tf_op jit(solution)/shard_map/gather/pallas_call | solution.py:144
  137.0 10.1 %fusion.38 = (bf16[1536,256]{0,1:T(8,128)(2,1)}, f32[1536,256]{0,1:T(8,128)}) fusion(bf16[1536,4096]{1,0:T(8,128)(2,1)} %bitcast.55, bf16[256,8192]{1,0:T(8,128)(2,1)} %param.11, s32[]{:T(128)S(6)} %select_n.2), kind=kOutput, calls=%fused_computation.65 | convolution fusion | flops 3221618688 | bytes 17039364 | tf_op jit(solution)/shard_map/dot_general | solution.py:21
  147.2 0.5 collective-permute-start
  147.7 0.1 constant_dynamic-slice_fusion
  147.8 8.1 %fusion.37 = (bf16[1536,256]{0,1:T(8,128)(2,1)}, f32[1536,256]{0,1:T(8,128)}) fusion(bf16[1536,4096]{1,0:T(8,128)(2,1)} %bitcast.51, bf16[4096,256]{1,0:T(8,128)(2,1)S(1)} %constant_dynamic-slice_fusion), kind=kOutput, calls=%fused_computation.64 | convolution fusion | flops 3221618688 | bytes 17039360 | tf_op jit(solution)/shard_map/dot_general | solution.py:285
  156.0 1.5 collective-permute-start.2
  157.7 8.8 %fusion.36 = (bf16[1536,256]{0,1:T(8,128)(2,1)}, f32[1536,256]{0,1:T(8,128)}) fusion(bf16[1536,4096]{1,0:T(8,128)(2,1)} %bitcast.52, bf16[4096,256]{1,0:T(8,128)(2,1)S(1)} %constant_dynamic-slice_fusion.1), kind=kOutput, calls=%fused_computation.63 | convolution fusion | flops 3221618688 | bytes 17039360 | tf_op jit(solution)/shard_map/dot_general | solution.py:286
  166.4 0.5 collective-permute-start.1
  166.9 0.4 convert_reduce_fusion
  167.3 33.7 %all-gather = f32[2,1,768]{2,1,0:T(1,128)S(1)} all-gather(f32[1,1,768]{2,1,0:T(1,128)S(1)} %reshape.76), channel_id=1, replica_groups=mesh['lang'=2,'fsdp'=16] {'lang'}, dimensions={0}, use_global_device_ids=true | all-gather | bytes 9216 | tf_op jit(solution)/shard_map/all_gather | solution.py:281
  201.1 4.0 %multiply_convert_fusion = (bf16[1536,256]{0,1:T(8,128)(2,1)S(1)}, bf16[1536,256]{0,1:T(8,128)(2,1)S(1)}, bf16[1536,256]{0,1:T(8,128)(2,1)S(1)}) fusion(f32[1536,256]{0,1:T(8,128)} %get-tuple-element.16, bf16[1536,256]{0,1:T(8,128)(2,1)} %collective-permute-done.1, f32[1536]{0:T(1024)S(1)} %reshape.77, f32[1536,256]{0,1:T(8,128)} %get-tuple-element.18, ...), kind=kLoop, calls=%fused_computation.37 | loop fusion | flops 9043968 | bytes 9443328 | tf_op jit(solution)/shard_map/convert_element_type | solution.py:290
  205.1 6.8 %multiply_reduce_fusion = (f32[256]{0:T(256)S(1)}, f32[256,4096]{1,0:T(8,128)}) fusion(bf16[2,768,4096]{2,1,0:T(8,128)(2,1)} %get-tuple-element.6, bf16[1536,256]{0,1:T(8,128)(2,1)S(1)} %get-tuple-element.8), kind=kOutput, calls=%fused_computation.25 | convolution fusion | flops 1612709632 | bytes 10880000 | tf_op jit(solution)/shard_map/dot_general | solution.py:15
  211.9 6.8 %multiply_reduce_fusion.3 = (f32[256]{0:T(256)S(1)}, f32[256,4096]{1,0:T(8,128)}) fusion(bf16[2,768,4096]{2,1,0:T(8,128)(2,1)} %get-tuple-element.6, bf16[1536,256]{0,1:T(8,128)(2,1)S(1)} %get-tuple-element.8), kind=kOutput, calls=%fused_computation.28 | convolution fusion | flops 1612709632 | bytes 10880000 | tf_op jit(solution)/shard_map/dot_general | solution.py:15
  218.8 3.8 %multiply_reduce_fusion.2 = (f32[256]{0:T(256)S(1)}, f32[4096,256]{1,0:T(8,128)}) fusion(bf16[1536,256]{0,1:T(8,128)(2,1)S(1)} %get-tuple-element.9, bf16[2,768,4096]{2,1,0:T(8,128)(2,1)S(1)} %bitcast.54), kind=kOutput, calls=%fused_computation.27 | convolution fusion | flops 1612709632 | bytes 10880000 | tf_op jit(solution)/shard_map/dot_general | solution.py:15
  222.6 3.9 %multiply_reduce_fusion.5 = (f32[256]{0:T(256)S(1)}, f32[4096,256]{1,0:T(8,128)}) fusion(bf16[1536,256]{0,1:T(8,128)(2,1)S(1)} %get-tuple-element.9, bf16[2,768,4096]{2,1,0:T(8,128)(2,1)S(1)} %bitcast.54), kind=kOutput, calls=%fused_computation.30 | convolution fusion | flops 1612709632 | bytes 10880000 | tf_op jit(solution)/shard_map/dot_general | solution.py:15
  226.6 3.8 %multiply_reduce_fusion.1 = (f32[256]{0:T(256)S(1)}, f32[4096,256]{1,0:T(8,128)}) fusion(bf16[1536,256]{0,1:T(8,128)(2,1)S(1)} %get-tuple-element.10, bf16[2,768,4096]{2,1,0:T(8,128)(2,1)S(1)} %bitcast.54), kind=kOutput, calls=%fused_computation.26 | convolution fusion | flops 1612709632 | bytes 10880000 | tf_op jit(solution)/shard_map/dot_general | solution.py:15
  230.4 3.8 %multiply_reduce_fusion.4 = (f32[256]{0:T(256)S(1)}, f32[4096,256]{1,0:T(8,128)}) fusion(bf16[1536,256]{0,1:T(8,128)(2,1)S(1)} %get-tuple-element.10, bf16[2,768,4096]{2,1,0:T(8,128)(2,1)S(1)} %bitcast.54), kind=kOutput, calls=%fused_computation.29 | convolution fusion | flops 1612709632 | bytes 10880000 | tf_op jit(solution)/shard_map/dot_general | solution.py:15
  234.2 9.8 %convolution_convert_fusion.part_ref = bf16[1536,4096]{1,0:T(8,128)(2,1)} fusion(bf16[4096,256]{1,0:T(8,128)(2,1)S(1)} %copy-done.4, bf16[4096,256]{1,0:T(8,128)(2,1)S(1)} %constant_dynamic-slice_fusion, bf16[1536,256]{0,1:T(8,128)(2,1)S(1)} %get-tuple-element.10, bf16[1536,256]{0,1:T(8,128)(2,1)S(1)} %get-tuple-element.9), kind=kOutput, calls=%fused_computation | convolution fusion | flops 6460276736 | bytes 18350080 | tf_op jit(solution)/shard_map/dot_general | solution.py:21
  244.0 4.9 %psum.7 = f32[2,256]{1,0:T(2,128)S(1)} all-reduce(f32[2,256]{1,0:T(2,128)S(1)} %pad_maximum_fusion), channel_id=1, replica_groups=mesh['lang'=2,'fsdp'=16] {'lang'}, use_global_device_ids=true, to_apply=%region_7.0 | all-reduce | flops 512 | bytes 4096 | tf_op jit(solution)/shard_map/psum | solution.py:313
  249.0 4.6 %copy-done = bf16[1536,4096]{1,0:T(8,128)(2,1)S(1)} copy-done((bf16[1536,4096]{1,0:T(8,128)(2,1)S(1)}, bf16[1536,4096]{1,0:T(8,128)(2,1)}, u32[]{:S(2)}) %copy-start) | copy-done | bytes 12582936
  253.6 76.7 %scatter.1 = bf16[48,8192]{1,0:T(8,128)(2,1)S(1)} custom-call(bf16[1536,4096]{1,0:T(8,128)(2,1)S(1)} %copy-done), custom_call_target="tpu_custom_call" | custom-call | tf_op jit(solution)/shard_map/scatter/pallas_call | solution.py:243
  330.3 2.5 add_convert_fusion
  332.8 9.1 %add_convert_fusion.1 = (bf16[4096,256]{1,0:T(8,128)(2,1)}, bf16[4096,256]{1,0:T(8,128)(2,1)}) fusion(f32[4096,256]{1,0:T(8,128)} %get-tuple-element.26, f32[4096,256]{1,0:T(8,128)} %get-tuple-element.32, f32[256]{0:T(256)S(1)} %bitcast.48, f32[256]{0:T(256)S(1)} %bitcast.46, f32[4096,256]{1,0:T(8,128)} %get-tuple-element.24, f32[4096,256]{1,0:T(8,128)} %get-tuple-element.30), kind=kLoop, calls=%fused_computation.23 | loop fusion | flops 8388608 | bytes 20973568 | tf_op jit(solution)/shard_map/convert_element_type | solution.py:321
  341.9 0.9 copy.11
  (37 shorter events, 0.3 us)
Async XLA Ops:
  137.0 10.7 %copy-start.5 = (bf16[8192,256]{1,0:T(8,128)(2,1)S(1)}, bf16[8192,256]{1,0:T(8,128)(2,1)}, u32[]{:S(2)}) copy-start(bf16[8192,256]{1,0:T(8,128)(2,1)} %param.9) | copy-start | bytes 12582916
  147.2 53.9 %collective-permute-start = (bf16[1536,256]{0,1:T(8,128)(2,1)}, bf16[1536,256]{0,1:T(8,128)(2,1)S(1)}, u32[]{:S(2)}, u32[]{:S(2)}) collective-permute-start(bf16[1536,256]{0,1:T(8,128)(2,1)} %get-tuple-element.19), channel_id=1, source_target_pairs={{0,16},{16,0},{1,17},{17,1},{2,18},{18,2},{3,19},{19,3},{4,20},{20... | collective-permute-start | bytes 2359304 | tf_op jit(solution)/shard_map/ppermute | solution.py:266
  147.8 9.7 %copy-start.6 = (bf16[8192,256]{1,0:T(8,128)(2,1)S(1)}, bf16[8192,256]{1,0:T(8,128)(2,1)}, u32[]{:S(2)}) copy-start(bf16[8192,256]{1,0:T(8,128)(2,1)} %param.10) | copy-start | bytes 12582916
  156.0 45.1 %collective-permute-start.2 = (bf16[1536,256]{0,1:T(8,128)(2,1)}, bf16[1536,256]{0,1:T(8,128)(2,1)}, u32[]{:S(2)}, u32[]{:S(2)}) collective-permute-start(bf16[1536,256]{0,1:T(8,128)(2,1)} %get-tuple-element.17), channel_id=1, source_target_pairs={{0,16},{16,0},{1,17},{17,1},{2,18},{18,2},{3,19},{19,3},{4,20},{20... | collective-permute-start | bytes 2359304 | tf_op jit(solution)/shard_map/ppermute | solution.py:266
  157.6 8.8 %copy-start.3 = (bf16[4096,256]{1,0:T(8,128)(2,1)}, bf16[4096,256]{1,0:T(8,128)(2,1)S(1)}, u32[]{:S(2)}) copy-start(bf16[4096,256]{1,0:T(8,128)(2,1)S(1)} %constant_dynamic-slice_fusion.1) | copy-start | bytes 6291460
  157.6 9.3 %copy-start.7 = (s32[1,768]{1,0:T(1,128)S(1)}, s32[1,768]{1,0:T(1,128)}, u32[]{:S(2)}) copy-start(s32[1,768]{1,0:T(1,128)} %param.8) | copy-start | bytes 9220
  166.4 34.7 %collective-permute-start.1 = (bf16[1536,256]{0,1:T(8,128)(2,1)}, bf16[1536,256]{0,1:T(8,128)(2,1)}, u32[]{:S(2)}, u32[]{:S(2)}) collective-permute-start(bf16[1536,256]{0,1:T(8,128)(2,1)} %get-tuple-element.15), channel_id=1, source_target_pairs={{0,16},{16,0},{1,17},{17,1},{2,18},{18,2},{3,19},{19,3},{4,20},{20... | collective-permute-start | bytes 2359304 | tf_op jit(solution)/shard_map/ppermute | solution.py:266
  205.1 13.6 %slice-start = ((s8[12582912]{0:T(1024)(128)(4,1)}), s8[4194304]{0:T(1024)(128)(4,1)S(1)}, s32[]{:S(2)}) async-start(s8[12582912]{0:T(1024)(128)(4,1)} %bitcast.53), calls=%async_computation | async-start | bytes 8388608
  205.1 13.6 %slice-start.1 = ((s8[12582912]{0:T(1024)(128)(4,1)}), s8[4194304]{0:T(1024)(128)(4,1)S(1)}, s32[]{:S(2)}) async-start(s8[12582912]{0:T(1024)(128)(4,1)} %bitcast.53), calls=%async_computation.1 | async-start | bytes 8388608
  211.9 6.8 %slice-start.2 = ((s8[12582912]{0:T(1024)(128)(4,1)}), s8[4194304]{0:T(1024)(128)(4,1)S(1)}, s32[]{:S(2)}) async-start(s8[12582912]{0:T(1024)(128)(4,1)} %bitcast.53), calls=%async_computation.2 | async-start | bytes 8388608
  230.4 3.8 %copy-start.4 = (bf16[4096,256]{1,0:T(8,128)(2,1)S(1)}, bf16[4096,256]{1,0:T(8,128)(2,1)}, u32[]{:S(2)}) copy-start(bf16[4096,256]{1,0:T(8,128)(2,1)} %copy-done.3) | copy-start | bytes 6291460
  249.0 4.6 %copy-start = (bf16[1536,4096]{1,0:T(8,128)(2,1)S(1)}, bf16[1536,4096]{1,0:T(8,128)(2,1)}, u32[]{:S(2)}) copy-start(bf16[1536,4096]{1,0:T(8,128)(2,1)} %convolution_convert_fusion.part_ref) | copy-start | bytes 37748740
  253.6 76.7 %copy-start.1 = (f32[256,4096]{1,0:T(8,128)S(1)}, f32[256,4096]{1,0:T(8,128)}, u32[]{:S(2)}) copy-start(f32[256,4096]{1,0:T(8,128)} %get-tuple-element.22) | copy-start | bytes 12582916
  253.6 76.7 %copy-start.2 = (f32[256,4096]{1,0:T(8,128)S(1)}, f32[256,4096]{1,0:T(8,128)}, u32[]{:S(2)}) copy-start(f32[256,4096]{1,0:T(8,128)} %get-tuple-element.28) | copy-start | bytes 12582916

commit v2 on v1

--- a/solution.py
+++ b/solution.py
@@ -9,6 +9,7 @@
 
 epsilon = 1e-06
 CORES = 2
+VMEM_ARRIVALS = 8 * 2**20
 
 
 def contract_rows(left, right):
@@ -34,12 +35,16 @@
 
 
 def gather_kernel(
-    langs, shards, tok_ref, up_ref, tok_out, up_out,
+    langs, shards, swaps, tok_ref, up_ref, wg_ref, wu_ref, wd_ref, inv_ref,
+    tok_out, up_out, pre_out, back_out, inv_out,
+    weights, down, feats, ups, pre_send, back_send, pre_recv, back_recv,
     ring_send, ring_recv, sib_send, sib_recv, lang_send, lang_recv, local_sem,
+    weight_sem, part_send, part_recv, inv_send, inv_recv,
 ):
     chips = shards // CORES
     rows = tok_ref.shape[0]
     width = tok_ref.shape[1] // langs
+    units = wg_ref.shape[1]
     lang = lax.axis_index("lang")
     me = lax.axis_index("fsdp")
     core = me % CORES
@@ -58,6 +63,9 @@
     ins = (tok_ref, up_ref)
     outs = (tok_out, up_out)
     nexts = (right, left)
+    sents = (pre_send, back_send)
+    recvs = (pre_recv, back_recv)
+    sums = (pre_out, back_out)
 
     def block(array, group, shard):
         return outs[array].at[group, pl.ds(pl.multiple_of(shard * rows, rows), rows), :]
@@ -71,13 +79,35 @@
             device_id=device, device_id_type=pl.DeviceIdType.MESH,
         )
 
-    def origin(array, step):
-        shift = chips - step if array == 0 else step
-        return chip_of((place + shift) % chips, chips) * CORES + core
-
-    sends = []
-    locals_ = []
-    lang_copies = {}
+    def chip_at(array, step):
+        shift = step if array else chips - step
+        return chip_of((place + shift) % chips, chips)
+
+    def group_at(d):
+        return (lang + langs - d) % langs
+
+    def ring_copy(array, d, step):
+        held = block(array, group_at(d), chip_at(array, step) * CORES + core)
+        return remote(
+            held, held, ring_send.at[array, d, step], ring_recv.at[array, d, step],
+            (lang, nexts[array]),
+        )
+
+    def sib_copy(array, d, step):
+        held = block(array, group_at(d), chip_at(array, step) * CORES + core)
+        return remote(
+            held, held, sib_send.at[array, d, step], sib_recv.at[array, d, step], (lang, sibling)
+        )
+
+    def part_copy(array, e, d, step):
+        group, chip = group_at(d), chip_at(array, step)
+        return remote(
+            sents[array].at[group, chip], recvs[array].at[e - 1, group, chip],
+            part_send.at[array, e, group, chip], part_recv.at[array, e, group, chip],
+            ((lang + e) % langs, me),
+        )
+
+    lang_copies, first, inv_copies = {}, [], []
     for array in range(2):
         for d in range(1, langs):
             peer = (lang + d) % langs
@@ -87,73 +117,142 @@
             )
             copy.start()
             lang_copies[array, d] = copy
-    for array in range(2):
-        copy = pltpu.make_async_copy(own(array, lang), block(array, lang, me), local_sem.at[array])
+        copy = pltpu.make_async_copy(own(array, lang), block(array, lang, me), local_sem.at[array, 0])
         copy.start()
-        locals_.append(copy)
-
-    ring = {}
-    sib = {}
-
-    def forward(array, d, step, src):
-        group = (lang + langs - d) % langs
-        shard = origin(array, step)
-        dst = block(array, group, shard)
-        if step < chips - 1:
-            copy = remote(
-                src, dst, ring_send.at[array, d, step], ring_recv.at[array, d, step],
-                (lang, nexts[array]),
+        first.append(copy)
+    for d in range(1, langs):
+        copy = remote(
+            inv_ref, inv_out.at[lang], inv_send.at[d], inv_recv.at[d], ((lang + d) % langs, me)
+        )
+        copy.start()
+        inv_copies.append(copy)
+    inv_out[lang] = inv_ref[...]
+    slab = pl.ds(pl.multiple_of(lang * width, width), width)
+    loads = [
+        pltpu.make_async_copy(wg_ref.at[slab, :], weights.at[:, pl.ds(0, units)], weight_sem.at[0]),
+        pltpu.make_async_copy(
+            wu_ref.at[slab, :], weights.at[:, pl.ds(units, units)], weight_sem.at[1]
+        ),
+        pltpu.make_async_copy(wd_ref.at[:, slab], down, weight_sem.at[2]),
+    ]
+
+    for d in range(langs):
+        for array in range(2):
+            if d == 0:
+                first[array].wait()
+            else:
+                lang_copies[array, d].wait_recv()
+            ring_copy(array, d, 0).start()
+            sib_copy(array, d, 0).start()
+    for copy in loads:
+        copy.start()
+    for copy in loads:
+        copy.wait()
+
+    def compute(step, d):
+        group = group_at(d)
+        fetches = []
+        for array in range(2):
+            sib_copy(array, d, step).wait_recv()
+            chip = chip_at(array, step)
+            pair = pl.ds(pl.multiple_of(chip * (CORES * rows), CORES * rows), CORES * rows)
+            copy = pltpu.make_async_copy(
+                outs[array].at[group, pair, :], (feats, ups)[array], local_sem.at[array, 1]
             )
             copy.start()
-            ring[array, d, step] = copy
-        copy = remote(
-            src, dst, sib_send.at[array, d, step], sib_recv.at[array, d, step], (lang, sibling)
-        )
-        copy.start()
-        sib[array, d, step] = copy
-
-    for step in range(chips):
+            fetches.append(copy)
+        for array in range(2):
+            fetches[array].wait()
+            chip = chip_at(array, step)
+            if array == 0:
+                value = jnp.dot(feats[...], weights[...], preferred_element_type=jnp.float32)
+            else:
+                value = contract_cols(ups[...], down[...])
+            sums[array][group, chip] = value
+            if swaps:
+                sents[array][group, chip] = value.astype(jnp.bfloat16)
+            for e in range(1, swaps + 1):
+                part_copy(array, e, d, step).start()
+
+    def advance(step, carry):
         for d in range(langs):
             for array in range(2):
-                group = (lang + langs - d) % langs
-                if step == 0:
-                    if d == 0:
-                        src = own(array, lang)
-                    else:
-                        lang_copies[array, d].wait_recv()
-                        src = block(array, group, me)
-                else:
-                    ring[array, d, step - 1].wait_recv()
-                    src = block(array, group, origin(array, step))
-                forward(array, d, step, src)
-    for copy in locals_:
-        copy.wait()
+                ring_copy(array, d, step - 1).wait_recv()
+
+                @pl.when(step < chips - 1)
+                def _():
+                    ring_copy(array, d, step).start()
+
+                sib_copy(array, d, step).start()
+            compute(step - 1, d)
+        return carry
+
+    lax.fori_loop(1, chips, advance, 0)
+    for d in range(langs):
+        compute(chips - 1, d)
+
+    def finish(step, carry):
+        for d in range(langs):
+            for array in range(2):
+                group, chip = group_at(d), chip_at(array, step)
+                for e in range(1, swaps + 1):
+                    part_copy(array, e, d, step).wait()
+                    sums[array][group, chip] += recvs[array][e - 1, group, chip].astype(jnp.float32)
+                sib_copy(array, d, step).wait_send()
+
+                @pl.when(step < chips - 1)
+                def _():
+                    ring_copy(array, d, step).wait_send()
+        return carry
+
+    lax.fori_loop(0, chips, finish, 0)
     for copy in lang_copies.values():
         copy.wait_send()
-    for copy in ring.values():
-        copy.wait_send()
-    for copy in sib.values():
+    for copy in inv_copies:
         copy.wait()
 
 
-def gather(tokens, grad_out, langs, shards):
-    rows, width = tokens.shape
+def gather(tokens, grad_out, w_gate, w_up, w_down, inverse, langs, shards, swaps):
+    rows, depth = tokens.shape
+    width = depth // langs
+    units = w_gate.shape[1]
     chips = shards // CORES
-    out = jax.ShapeDtypeStruct((langs, rows * shards, width // langs), tokens.dtype)
+    pair = CORES * rows
+    held = (langs, chips, pair) if swaps else (1, 1, pair)
+    out = jax.ShapeDtypeStruct((langs, rows * shards, width), tokens.dtype)
     dma = pltpu.SemaphoreType.DMA
+    any_space = pl.BlockSpec(memory_space=pl.ANY)
+    vmem = pl.BlockSpec(memory_space=pltpu.VMEM)
     return pl.pallas_call(
-        functools.partial(gather_kernel, langs, shards),
-        out_shape=(out, out),
-        in_specs=[pl.BlockSpec(memory_space=pl.ANY)] * 2,
-        out_specs=(pl.BlockSpec(memory_space=pl.ANY),) * 2,
+        functools.partial(gather_kernel, langs, shards, swaps),
+        out_shape=(
+            out, out,
+            jax.ShapeDtypeStruct((langs, chips, pair, 2 * units), jnp.float32),
+            jax.ShapeDtypeStruct((langs, chips, pair, units), jnp.float32),
+            jax.ShapeDtypeStruct((langs,) + inverse.shape, jnp.float32),
+        ),
+        in_specs=[any_space] * 5 + [vmem],
+        out_specs=(any_space, any_space, vmem, vmem, vmem),
         scratch_shapes=[
+            pltpu.VMEM((width, 2 * units), w_gate.dtype),
+            pltpu.VMEM((units, width), w_down.dtype),
+            pltpu.VMEM((pair, width), tokens.dtype),
+            pltpu.VMEM((pair, width), tokens.dtype),
+            pltpu.VMEM(held + (2 * units,), jnp.bfloat16),
+            pltpu.VMEM(held + (units,), jnp.bfloat16),
+            pltpu.VMEM((max(swaps, 1),) + held + (2 * units,), jnp.bfloat16),
+            pltpu.VMEM((max(swaps, 1),) + held + (units,), jnp.bfloat16),
             dma((2, langs, chips)), dma((2, langs, chips)),
             dma((2, langs, chips)), dma((2, langs, chips)),
-            dma((2, langs)), dma((2, langs)), dma((2,)),
+            dma((2, langs)), dma((2, langs)), dma((2, 2)), dma((3,)),
+            dma((2, langs, langs, chips)), dma((2, langs, langs, chips)),
+            dma((langs,)), dma((langs,)),
         ],
-        compiler_params=pltpu.CompilerParams(collective_id=0, has_side_effects=True),
+        compiler_params=pltpu.CompilerParams(
+            collective_id=0, has_side_effects=True, vmem_limit_bytes=48 * 2**20
+        ),
         name="gather",
-    )(tokens, grad_out)
+    )(tokens, grad_out, w_gate, w_up, w_down, inverse)
 
 
 def scatter_kernel(
@@ -272,19 +371,25 @@
     lang = lax.axis_index("lang")
     depth = w_gate.shape[0]
     width = depth // langs
-    feats, ups = gather(tokens[0], grad_out[0], langs, shards)
+    segment = doc_ids[0]
+    counts = jnp.sum((segment[:, None] == segment[None, :]).astype(jnp.float32), axis=1)
+    units = w_gate.shape[1]
+    arrives = (langs - 1) * langs * tokens.shape[1] * shards * 3 * units * 2
+    swaps = langs - 1 if arrives <= VMEM_ARRIVALS else 0
+    feats, ups, pre, back, inverse = gather(
+        tokens[0], grad_out[0], w_gate, w_up, w_down, (1.0 / counts)[None], langs, shards, swaps
+    )
+    if not swaps:
+        pre, back = swap_sum(pre, langs), swap_sum(back, langs)
     count_tokens = feats.shape[1]
     feats = feats.reshape(langs * count_tokens, width)
     ups = ups.reshape(langs * count_tokens, width)
-    segment = doc_ids[0]
-    counts = jnp.sum((segment[:, None] == segment[None, :]).astype(jnp.float32), axis=1)
-    inverse = lax.all_gather(1.0 / counts, "lang", axis=0, tiled=True)[:, None]
+    inverse = inverse.reshape(-1)[:, None]
     wg = lax.dynamic_slice_in_dim(w_gate, lang * width, width, 0)
     wu = lax.dynamic_slice_in_dim(w_up, lang * width, width, 0)
-    wd = lax.dynamic_slice_in_dim(w_down, lang * width, width, 1)
-    gate_pre = swap_sum(jnp.dot(feats, wg, preferred_element_type=jnp.float32), langs)
-    up_pre = swap_sum(jnp.dot(feats, wu, preferred_element_type=jnp.float32), langs)
-    hid_grad = swap_sum(contract_cols(ups, wd), langs) * inverse
+    pre = pre.reshape(-1, 2 * units)
+    gate_pre, up_pre = pre[:, :units], pre[:, units:]
+    hid_grad = back.reshape(-1, units) * inverse
     gate_sig = jax.nn.sigmoid(gate_pre)
     activated = gate_pre * gate_sig
     hidden = (activated * up_pre * inverse).astype(jnp.bfloat16)

time: 343 us -> 298 us (0.87)
  blocking collectives: 38.7 us -> 4.94 us
  matrix products: 65.8 us -> 36.6 us
  Pallas kernels: 213 us -> 229 us
  local copies, waits for them, and re-layouts: 5.79 us -> 10.6 us
    all_gather x1 -> x0, blocking collectives: 33.7 us -> none  [body(): inverse = lax.all_gather(1.0 / counts, 'lang', axis=0, tiled=True)[:, None]]
    dot_general x2 -> x0, matrix products: 16.9 us -> none  [the longest x1 8.75 us: body(): jnp.dot(feats, wu, preferred_element_type=jnp.float32)]
    pallas_call x1, Pallas kernels: 136 us -> 150 us  [gather(): pl.pallas_call(functools.partial(gather_kernel, langs, shards, swaps), ou...]
    dot_general x2 -> x1, matrix products: 19.9 us -> 9.67 us  [contract_cols(): lax.dot_general(left, right, (((1,), (1,)), ((), ())), preferred_element_...]
    dynamic_slice x1, local copies, waits for them, and re-layouts: 0.14 us -> 4.56 us  [body(): wu = lax.dynamic_slice_in_dim(w_up, lang * width, width, 0)]
  transfers between devices with their start and end apart: 3 -> 0, of which waited for: 0 -> 0; matrix products, arithmetic and copies ran while one was open for 5% -> 0% of each run, Pallas kernels for 0% -> 0%
where the time goes in v2:
time: 298 us
  Pallas kernels  229 us (77%)
  matrix products  36.6 us (12%)
  other arithmetic  16.1 us (5%)
  local copies, waits for them, and re-layouts  10.6 us (4%)
  blocking collectives  4.94 us (2%)
    pallas_call x1, Pallas kernels, gather(): pl.pallas_call(functools.partial(gather_kernel, langs, shards, swaps), ou...  150 us
    pallas_call x1, Pallas kernels, scatter(): pl.pallas_call(functools.partial(scatter_kernel, langs, shards), out_shap...  78.6 us
    dot_general x6, matrix products, contract_rows(): lax.dot_general(left, right, (((0,), (0,)), ((), ())), preferred_element_...  26.9 us
    convert_element_type x2, other arithmetic, weigh(): return total.astype(jnp.bfloat16)  11.8 us
    dot_general x1, matrix products, contract_cols(): lax.dot_general(left, right, (((1,), (1,)), ((), ())), preferred_element_...  9.67 us
    unnamed x27, local copies, waits for them, and re-layouts  6.07 us

profile of v2, /device:TPU:0, one launch (start us, length us, event | category | flops | bytes accessed | tf_op | source)
XLA Modules:
  0.0 297.8 jit_solution(14819068363502723465)
XLA Ops:
  0.6 0.7 reduce
  1.3 0.4 convert_reduce_fusion
  1.7 0.0 copy-start.1
  1.7 0.0 copy-start.2
  1.8 4.6 %constant_dynamic-slice_fusion = (bf16[4096,256]{1,0:T(8,128)(2,1)}, bf16[4096,256]{1,0:T(8,128)(2,1)}) fusion(bf16[8192,256]{1,0:T(8,128)(2,1)} %wu_ref.1, s32[]{:T(128)S(6)} %select_n.4, bf16[8192,256]{1,0:T(8,128)(2,1)} %wg_ref.1), kind=kLoop, calls=%fused_computation.54 | loop fusion | bytes 8388612 | tf_op jit(solution)/shard_map/dynamic_slice | solution.py:389
  6.3 150.1 %gather.1 = (bf16[2,768,4096]{2,1,0:T(8,128)(2,1)}, bf16[2,768,4096]{2,1,0:T(8,128)(2,1)}, f32[2,8,96,512]{3,2,1,0:T(8,128)}, f32[2,8,96,256]{3,2,1,0:T(8,128)S(1)}, f32[2,1,768]{2,1,0:T(1,128)S(1)}) custom-call(bf16[48,8192]{1,0:T(8,128)(2,1)S(1)} %bitcast.43, bf16[48,8192]{1,0:T(8,128)(2,1)S(1)} %bitcast.44, bf16[8192,256]{1,0:T(8,128)(2,1)} %wg_ref.1, ...), custom_call_target="tpu_custom_call" | custom-call | tf_op jit(solution)/shard_map/gather/pallas_call | solution.py:226
  156.5 3.1 %multiply_convert_fusion.2 = (bf16[1536,256]{1,0:T(8,128)(2,1)S(1)}, bf16[1536,256]{1,0:T(8,128)(2,1)S(1)}, bf16[1536,256]{1,0:T(8,128)(2,1)S(1)}) fusion(f32[2,8,96,256]{3,2,1,0:T(8,128)S(1)} %get-tuple-element.9, f32[1536,512]{1,0:T(8,128)} %bitcast.45, f32[1536]{0:T(1024)S(1)} %mul.89), kind=kLoop, calls=%fused_computation.38 | loop fusion | flops 6684672 | bytes 7084032 | tf_op jit(solution)/shard_map/convert_element_type | solution.py:396
  159.6 0.0 copy-start.7
  159.7 0.0 slice-start
  159.7 7.7 %multiply_reduce_fusion = (f32[256]{0:T(256)S(1)}, f32[256,4096]{1,0:T(8,128)}) fusion(bf16[2,768,4096]{2,1,0:T(8,128)(2,1)} %get-tuple-element.13, bf16[1536,256]{1,0:T(8,128)(2,1)S(1)} %get-tuple-element.16), kind=kOutput, calls=%fused_computation.25 | convolution fusion | flops 1612709632 | bytes 10880000 | tf_op jit(solution)/shard_map/dot_general | solution.py:16
  167.4 3.8 %multiply_reduce_fusion.3 = (f32[256]{0:T(256)S(1)}, f32[256,4096]{1,0:T(8,128)}) fusion(bf16[2,768,4096]{2,1,0:T(8,128)(2,1)S(1)} %copy-done.9, bf16[1536,256]{1,0:T(8,128)(2,1)S(1)} %get-tuple-element.16), kind=kOutput, calls=%fused_computation.28 | convolution fusion | flops 1612709632 | bytes 10880000 | tf_op jit(solution)/shard_map/dot_general | solution.py:16
  171.2 3.8 %multiply_reduce_fusion.2 = (f32[256]{0:T(256)S(1)}, f32[4096,256]{1,0:T(8,128)}) fusion(bf16[1536,256]{1,0:T(8,128)(2,1)S(1)} %get-tuple-element.14, bf16[2,768,4096]{2,1,0:T(8,128)(2,1)S(1)} %bitcast.53), kind=kOutput, calls=%fused_computation.27 | convolution fusion | flops 1612709632 | bytes 10880000 | tf_op jit(solution)/shard_map/dot_general | solution.py:16
  175.0 3.8 %multiply_reduce_fusion.5 = (f32[256]{0:T(256)S(1)}, f32[4096,256]{1,0:T(8,128)}) fusion(bf16[1536,256]{1,0:T(8,128)(2,1)S(1)} %get-tuple-element.14, bf16[2,768,4096]{2,1,0:T(8,128)(2,1)S(1)} %bitcast.53), kind=kOutput, calls=%fused_computation.30 | convolution fusion | flops 1612709632 | bytes 10880000 | tf_op jit(solution)/shard_map/dot_general | solution.py:16
  178.8 3.8 %multiply_reduce_fusion.1 = (f32[256]{0:T(256)S(1)}, f32[4096,256]{1,0:T(8,128)}) fusion(bf16[1536,256]{1,0:T(8,128)(2,1)S(1)} %get-tuple-element.15, bf16[2,768,4096]{2,1,0:T(8,128)(2,1)S(1)} %bitcast.53), kind=kOutput, calls=%fused_computation.26 | convolution fusion | flops 1612709632 | bytes 10880000 | tf_op jit(solution)/shard_map/dot_general | solution.py:16
  182.6 4.1 %multiply_reduce_fusion.4 = (f32[256]{0:T(256)S(1)}, f32[4096,256]{1,0:T(8,128)}) fusion(bf16[1536,256]{1,0:T(8,128)(2,1)S(1)} %get-tuple-element.15, bf16[2,768,4096]{2,1,0:T(8,128)(2,1)S(1)} %bitcast.53), kind=kOutput, calls=%fused_computation.29 | convolution fusion | flops 1612709632 | bytes 10880000 | tf_op jit(solution)/shard_map/dot_general | solution.py:16
  186.7 4.9 %psum.7 = f32[2,256]{1,0:T(2,128)S(1)} all-reduce(f32[2,256]{1,0:T(2,128)S(1)} %pad_maximum_fusion), channel_id=1, replica_groups=mesh['lang'=2,'fsdp'=16] {'lang'}, use_global_device_ids=true, to_apply=%region_7.0 | all-reduce | flops 512 | bytes 4096 | tf_op jit(solution)/shard_map/psum | solution.py:418
  191.7 9.3 %add_convert_fusion.1 = (bf16[4096,256]{1,0:T(8,128)(2,1)}, bf16[4096,256]{1,0:T(8,128)(2,1)}) fusion(f32[4096,256]{1,0:T(8,128)} %get-tuple-element.26, f32[4096,256]{1,0:T(8,128)} %get-tuple-element.32, f32[256]{0:T(256)S(1)} %bitcast.48, f32[256]{0:T(256)S(1)} %bitcast.46, f32[4096,256]{1,0:T(8,128)} %get-tuple-element.24, f32[4096,256]{1,0:T(8,128)} %get-tuple-element.30), kind=kLoop, calls=%fused_computation.23 | loop fusion | flops 8388608 | bytes 20973568 | tf_op jit(solution)/shard_map/convert_element_type | solution.py:426
  201.0 0.0 copy-start.8
  201.0 2.5 add_convert_fusion
  203.5 0.6 copy-done.8
  204.1 9.7 %convolution_convert_fusion.part_ref = bf16[1536,4096]{1,0:T(8,128)(2,1)} fusion(bf16[4096,256]{1,0:T(8,128)(2,1)S(1)} %copy-done.5, bf16[4096,256]{1,0:T(8,128)(2,1)S(1)} %copy-done.6, bf16[1536,256]{1,0:T(8,128)(2,1)S(1)} %copy-done.8, bf16[1536,256]{1,0:T(8,128)(2,1)S(1)} %get-tuple-element.14), kind=kOutput, calls=%fused_computation | convolution fusion | flops 6460276736 | bytes 18350080 | tf_op jit(solution)/shard_map/dot_general | solution.py:22
  213.7 4.6 %copy-done = bf16[1536,4096]{1,0:T(8,128)(2,1)S(1)} copy-done((bf16[1536,4096]{1,0:T(8,128)(2,1)S(1)}, bf16[1536,4096]{1,0:T(8,128)(2,1)}, u32[]{:S(2)}) %copy-start) | copy-done | bytes 12582936
  218.3 78.6 %scatter.1 = bf16[48,8192]{1,0:T(8,128)(2,1)S(1)} custom-call(bf16[1536,4096]{1,0:T(8,128)(2,1)S(1)} %copy-done), custom_call_target="tpu_custom_call" | custom-call | tf_op jit(solution)/shard_map/scatter/pallas_call | solution.py:342
  296.9 0.9 copy.11
  (30 shorter events, 0.2 us)
Async XLA Ops:
  1.7 4.6 %copy-start.1 = (bf16[1,48,8192]{2,1,0:T(8,128)(2,1)S(1)}, bf16[1,48,8192]{2,1,0:T(8,128)(2,1)}, u32[]{:S(2)}) copy-start(bf16[1,48,8192]{2,1,0:T(8,128)(2,1)} %param.6) | copy-start | bytes 2359300
  1.7 4.6 %copy-start.2 = (bf16[1,48,8192]{2,1,0:T(8,128)(2,1)S(1)}, bf16[1,48,8192]{2,1,0:T(8,128)(2,1)}, u32[]{:S(2)}) copy-start(bf16[1,48,8192]{2,1,0:T(8,128)(2,1)} %param.7) | copy-start | bytes 2359300
  156.5 10.9 %copy-start.9 = (bf16[2,768,4096]{2,1,0:T(8,128)(2,1)S(1)}, bf16[2,768,4096]{2,1,0:T(8,128)(2,1)}, u32[]{:S(2)}) copy-start(bf16[2,768,4096]{2,1,0:T(8,128)(2,1)} %get-tuple-element.13) | copy-start | bytes 37748740
  159.6 22.9 %copy-start.7 = (bf16[1536,256]{1,0:T(8,128)(2,1)}, bf16[1536,256]{1,0:T(8,128)(2,1)S(1)}, u32[]{:S(2)}) copy-start(bf16[1536,256]{1,0:T(8,128)(2,1)S(1)} %get-tuple-element.15) | copy-start | bytes 2359300
  159.7 11.5 %slice-start = ((s8[12582912]{0:T(1024)(128)(4,1)}), s8[4194304]{0:T(1024)(128)(4,1)S(1)}, s32[]{:S(2)}) async-start(s8[12582912]{0:T(1024)(128)(4,1)} %bitcast.52), calls=%async_computation | async-start | bytes 8388608
  159.7 11.5 %slice-start.1 = ((s8[12582912]{0:T(1024)(128)(4,1)}), s8[4194304]{0:T(1024)(128)(4,1)S(1)}, s32[]{:S(2)}) async-start(s8[12582912]{0:T(1024)(128)(4,1)} %bitcast.52), calls=%async_computation.1 | async-start | bytes 8388608
  167.4 3.8 %slice-start.2 = ((s8[12582912]{0:T(1024)(128)(4,1)}), s8[4194304]{0:T(1024)(128)(4,1)S(1)}, s32[]{:S(2)}) async-start(s8[12582912]{0:T(1024)(128)(4,1)} %bitcast.52), calls=%async_computation.2 | async-start | bytes 8388608
  191.7 9.3 %copy-start.3 = (f32[256,4096]{1,0:T(8,128)S(1)}, f32[256,4096]{1,0:T(8,128)}, u32[]{:S(2)}) copy-start(f32[256,4096]{1,0:T(8,128)} %get-tuple-element.22) | copy-start | bytes 12582916
  191.7 9.3 %copy-start.4 = (f32[256,4096]{1,0:T(8,128)S(1)}, f32[256,4096]{1,0:T(8,128)}, u32[]{:S(2)}) copy-start(f32[256,4096]{1,0:T(8,128)} %get-tuple-element.28) | copy-start | bytes 12582916
  201.0 2.5 copy-start.5
  201.0 2.5 copy-start.6
  201.0 3.1 %copy-start.8 = (bf16[1536,256]{1,0:T(8,128)(2,1)S(1)}, bf16[1536,256]{1,0:T(8,128)(2,1)}, u32[]{:S(2)}) copy-start(bf16[1536,256]{1,0:T(8,128)(2,1)} %copy-done.7) | copy-start | bytes 2359300
  213.7 4.6 %copy-start = (bf16[1536,4096]{1,0:T(8,128)(2,1)S(1)}, bf16[1536,4096]{1,0:T(8,128)(2,1)}, u32[]{:S(2)}) copy-start(bf16[1536,4096]{1,0:T(8,128)(2,1)} %convolution_convert_fusion.part_ref) | copy-start | bytes 37748740
